TPU v7x, 32 devices: a whole 2x2x4 slice. The times are simulated.
32 devices in a mesh: sec: 4 (over y, core), dp: 8 (over z, x), mp: 1.
Axes of the slice: x: 2, y: 2, z: 4, core: 2. Of those that a mesh axis runs over, the one named last changes fastest.
Arguments:
- patches: bfloat16 [320, 5120], P('dp'), may hold values from -6 to 6
- ln_gain: bfloat16 [1280], replicated, may hold values from 0.099609375 to 1.8984375
- ln_shift: bfloat16 [1280], replicated, may hold values from -3 to 3
- w_in: bfloat16 [5120, 5120], P('dp', ('sec', 'mp')), may hold values from -0.078125 to 0.078125
- b_in: bfloat16 [5120], P(('sec', 'mp')), may hold values from -3 to 3
- w_out: bfloat16 [5120, 8192], P(('sec', 'mp'), 'dp'), may hold values from -0.125 to 0.125
- b_out: bfloat16 [8192], P(('sec', 'mp')), may hold values from -3 to 3
- place: int32 [320], P('dp'), may hold values from 0 to 255, as said below
- image_counts: int32 [8], P('dp'), may hold values from 1 to 40, 128 in all
- text_rows: bfloat16 [2048, 8192], P('dp', ('sec', 'mp')), may hold values from -6 to 6
- segments: int32 [8, 256], P('dp'), may hold values from 0 to 3, never falling along the last dimension, each value on 1 to 128 neighbouring positions
- norm_gain: bfloat16 [2, 8192], replicated, may hold values from 0.099609375 to 1.8984375
- q_weight: bfloat16 [2, 8192, 4096], P(None, None, ('sec', 'mp'))
- kv_weight: bfloat16 [2, 2, 512, 8192], P(None, None, ('sec', 'mp'))
- o_weight: bfloat16 [2, 4096, 8192], P(None, ('sec', 'mp')), may hold values from -0.125 to 0.125
- grad_rows: bfloat16 [320, 8192], P('dp'), may hold values from -6 to 6
Outputs:
- final_rows: float32 [2048, 8192], P('dp', ('sec', 'mp'))
- patch_grads: float32 [320, 5120], P('dp')
Inputs may be any that keep to these rules, and one draw needn't show every extreme that they name: `place`: each owner's 40 entries are distinct token positions of its own packed sequence; only an owner's first image_counts entries are used. `image_counts`: the counts sum to 8 * (16) over all owners.
All inputs are finite; a program needn't handle non-finite values. No bound on the sum of `image_counts` on one device may be relied on, other than what follows from the above.
Results may differ from a plain program's by a relative error of at most 0.0055.
Values may be sent and summed in bfloat16 or wider, within the bound.
No kernel may reach another device: no remote copies, remote signals or barrier semaphores. Data moves between devices by JAX's collectives and lax.ppermute only.
A program may use at most 256 MiB of HBM per device.

v0:
```python
import math

import jax
import jax.numpy as jnp
from jax import lax
from jax.sharding import PartitionSpec as P

D = 8192
HEAD_DIM = 128


ln_eps = 1e-06
rms_eps = 1e-06
rope_base = 1000000.0


def group_norm(patch_rows, ln_gain, ln_shift):
    row_count = patch_rows.shape[0]
    grouped = patch_rows.astype(jnp.float32).reshape(row_count, -1, ln_gain.shape[0])
    center = grouped - jnp.mean(grouped, axis=-1, keepdims=True)
    spread = jnp.mean(center * center, axis=-1, keepdims=True)
    scaled = center * lax.rsqrt(spread + ln_eps) * ln_gain.astype(jnp.float32) + ln_shift.astype(
        jnp.float32
    )
    return scaled.reshape(row_count, -1)


def gelu_exact(values):
    return jax.nn.gelu(values, approximate=False)


def rotate(values, positions):
    head_depth = values.shape[-1]
    half_depth = head_depth // 2
    inv_freq = rope_base ** (-2.0 * jnp.arange(half_depth, dtype=jnp.float32) / head_depth)
    angles = positions[:, None] * inv_freq[None, :]
    cosine = jnp.cos(angles)[:, None, :]
    sine_part = jnp.sin(angles)[:, None, :]
    first_half = values[..., :half_depth]
    second = values[..., half_depth:]
    return jnp.concatenate(
        [first_half * cosine - second * sine_part, second * cosine + first_half * sine_part],
        axis=-1,
    )


def doc_mask(segment_ids):
    token_index = jnp.arange(segment_ids.shape[0], dtype=jnp.int32)
    same_doc = segment_ids[:, None] == segment_ids[None, :]
    allowed = same_doc & (token_index[None, :] <= token_index[:, None])
    positions = jnp.sum(allowed.astype(jnp.int32), axis=1) - 1
    return (allowed, positions.astype(jnp.float32))


def attend(normed, allowed, positions, q_local, kv_local):
    token_count = normed.shape[0]
    queries = jnp.dot(normed, q_local, preferred_element_type=jnp.float32).reshape(
        token_count, -1, HEAD_DIM
    )
    key_value = jnp.einsum("td,kcd->tkc", normed, kv_local, preferred_element_type=jnp.float32)
    key_value = lax.all_gather(key_value, "mp", axis=2, tiled=True)
    key_rows = rotate(key_value[:, 0:1, :], positions)[:, 0, :].astype(jnp.bfloat16)
    value_rows = key_value[:, 1, :].astype(jnp.bfloat16)
    queries = rotate(queries, positions).astype(jnp.bfloat16)
    scores = jnp.einsum("thd,sd->hts", queries, key_rows, preferred_element_type=jnp.float32) * (
        1.0 / math.sqrt(HEAD_DIM)
    )
    scores = jnp.where(allowed[None], scores, -jnp.inf)
    row_max = jnp.max(scores, axis=-1, keepdims=True)
    exp_scores = jnp.exp(scores - row_max)
    attn_weights = (exp_scores / jnp.sum(exp_scores, axis=-1, keepdims=True)).astype(jnp.bfloat16)
    attended = jnp.einsum(
        "hts,sd->thd", attn_weights, value_rows, preferred_element_type=jnp.float32
    )
    return attended.astype(jnp.bfloat16).reshape(token_count, -1)


def gather_features(rows_local):
    return lax.all_gather(rows_local, ("sec", "mp"), axis=1, tiled=True)


def section_features(rows_local, gain_row, allowed, positions, q_local, kv_local, o_local):
    share = rows_local.shape[1]
    square_sums = lax.psum(jnp.sum(rows_local * rows_local, axis=1), ("sec", "mp"))
    factor = lax.rsqrt(square_sums / D + rms_eps)
    gain_local = lax.dynamic_slice_in_dim(
        gain_row, lax.axis_index(("sec", "mp")) * share, share, 0
    ).astype(jnp.float32)
    normed_local = (rows_local * factor[:, None] * gain_local[None, :]).astype(jnp.bfloat16)
    normed = gather_features(normed_local)
    attended = attend(normed, allowed, positions, q_local, kv_local)
    summed = lax.psum_scatter(
        lax.dot_general(
            o_local, attended, (((0,), (1,)), ((), ())), preferred_element_type=jnp.float32
        ),
        ("sec", "mp"),
        scatter_dimension=0,
        tiled=True,
    )
    return rows_local + summed.T


def merger_front(patch_rows, ln_gain, ln_shift, w_in_full, b_in, w_out_full, b_out):
    normed = group_norm(patch_rows, ln_gain, ln_shift).astype(jnp.bfloat16)
    pre_act = jnp.dot(normed, w_in_full, preferred_element_type=jnp.float32) + b_in.astype(
        jnp.float32
    )
    hidden_units = gelu_exact(pre_act).astype(jnp.bfloat16)
    partial_out = jnp.dot(hidden_units, w_out_full, preferred_element_type=jnp.float32)
    merged = lax.psum_scatter(
        partial_out, ("sec", "mp"), scatter_dimension=1, tiled=True
    ) + b_out.astype(jnp.float32)
    return (merged.astype(jnp.bfloat16), pre_act)


def merger_back(patch_rows, pre_act, hidden_grads, ln_gain, ln_shift, w_in_full):
    _, pull_gelu = jax.vjp(gelu_exact, pre_act)
    pre_grads = pull_gelu(hidden_grads)[0].astype(jnp.bfloat16)
    normed_grads = lax.dot_general(
        pre_grads, w_in_full, (((1,), (1,)), ((), ())), preferred_element_type=jnp.float32
    )
    normed_grads = lax.psum(normed_grads, ("sec", "mp"))
    _, pull_norm = jax.vjp(
        lambda values: group_norm(values, ln_gain, ln_shift), patch_rows.astype(jnp.float32)
    )
    return pull_norm(normed_grads)[0]


def local(
    patches,
    ln_gain,
    ln_shift,
    w_in,
    b_in,
    w_out,
    b_out,
    place,
    image_counts,
    text_rows,
    segments,
    norm_gain,
    q_weight,
    kv_weight,
    o_weight,
    grad_rows,
):
    w_in_full, w_out_full = (
        lax.all_gather(w_in, "dp", axis=0, tiled=True),
        lax.all_gather(w_out, "dp", axis=1, tiled=True),
    )
    slot_count = patches.shape[0]
    tokens = text_rows.shape[0]
    slot_index = jnp.arange(slot_count, dtype=jnp.int32)
    live_slot = slot_index < image_counts[0]
    slot_grads = jnp.where(live_slot[:, None], grad_rows, jnp.zeros_like(grad_rows))
    hidden_grads = lax.dot_general(
        slot_grads, w_out_full, (((1,), (1,)), ((), ())), preferred_element_type=jnp.float32
    )
    merged_local, pre_act = merger_front(
        patches, ln_gain, ln_shift, w_in_full, b_in, w_out_full, b_out
    )
    patch_grads = merger_back(patches, pre_act, hidden_grads, ln_gain, ln_shift, w_in_full)
    token_index = jnp.arange(tokens, dtype=jnp.int32)
    select = (place[:, None] == token_index[None, :]) & live_slot[:, None]
    is_image = jnp.any(select, axis=0)
    picked = lax.dot_general(
        select.astype(jnp.bfloat16),
        merged_local,
        (((0,), (0,)), ((), ())),
        preferred_element_type=jnp.float32,
    )
    start_rows = jnp.where(is_image[:, None], picked, text_rows.astype(jnp.float32)).astype(
        jnp.bfloat16
    )
    allowed, positions = doc_mask(segments[0])
    layer_count = q_weight.shape[0]
    current = start_rows.astype(jnp.float32)
    for layer_index in range(layer_count):
        current = section_features(
            current,
            norm_gain[layer_index],
            allowed,
            positions,
            q_weight[layer_index],
            kv_weight[layer_index],
            o_weight[layer_index],
        )
    return (current, patch_grads)


def solution(mesh):
    in_specs = (
        P("dp", None),
        P(),
        P(),
        P("dp", ("sec", "mp")),
        P(("sec", "mp")),
        P(("sec", "mp"), "dp"),
        P(("sec", "mp")),
        P("dp"),
        P("dp"),
        P("dp", ("sec", "mp")),
        P("dp", None),
        P(),
        P(None, None, ("sec", "mp")),
        P(None, None, ("sec", "mp"), None),
        P(None, ("sec", "mp"), None),
        P("dp", None),
    )
    out_specs = (P("dp", ("sec", "mp")), P("dp", None))
    return jax.shard_map(local, mesh=mesh, in_specs=in_specs, out_specs=out_specs, check_vma=False)
```

profile of v0, /device:TPU:0, one launch (start us, length us, event | category | flops | bytes accessed | tf_op | source)
XLA Modules:
  0.0 970.3 jit_solution(1489968353549882613)
XLA Ops:
  7.3 0.7 all-gather.5.cloned.1.call-update
  8.0 0.7 all-gather.7.cloned.1.call-update
  8.9 0.4 reshape.223
  9.3 0.2 reduce_sum.78
  9.5 0.4 multiply_reduce_fusion.2
  10.5 185.3 %all-gather.5.cloned.1.call-done = bf16[5120,1280]{1,0:T(8,128)(2,1)} async-done(((bf16[640,1280]{1,0:T(8,128)(2,1)}), bf16[5120,1280]{1,0:T(8,128)(2,1)}) %all-gather.5.cloned.1.call-update) | async-done | bytes 13107216 | tf_op jit(solution)/shard_map/all_gather | solution.py:148
  195.8 7.1 convolution_add_fusion
  202.9 394.4 %all-gather.7.cloned.1.call-done = bf16[1280,8192]{1,0:T(8,128)(2,1)} async-done(((bf16[1280,1024]{1,0:T(8,128)(2,1)}), bf16[1280,8192]{1,0:T(8,128)(2,1)}) %all-gather.7.cloned.1.call-update) | async-done | bytes 20971536 | tf_op jit(solution)/shard_map/all_gather | solution.py:149
  597.3 12.1 %fusion.77 = f32[40,8192]{1,0:T(8,128)} fusion(bf16[1280,8192]{1,0:T(8,128)(2,1)} %all-gather.7.cloned.1.call-done, f32[40,1280]{1,0:T(8,128)S(1)} %convolution_add_fusion), kind=kOutput, calls=%fused_computation.105 | convolution fusion | flops 842188800 | bytes 22487040 | tf_op jit(solution)/shard_map/dot_general | solution.py:109
  610.4 25.7 %reduce-scatter.4.cloned.1.call-done = f32[40,2048]{1,0:T(8,128)} async-done(((f32[40,8192]{1,0:T(8,128)}), f32[40,2048]{1,0:T(8,128)}) %reduce-scatter.4.cloned.1.call-update) | async-done | bytes 327696 | tf_op jit(solution)/shard_map/reduce_scatter | solution.py:110
  636.1 2.0 fusion.27
  638.2 5.8 psum.21
  643.9 1.3 fusion.29
  645.3 0.2 reduce-scatter.6.cloned.1.call-start
  645.5 23.3 %slice_bitcast_fusion.1 = (bf16[1024,8192]{0,1:T(8,128)(2,1)}, bf16[1024,8192]{0,1:T(8,128)(2,1)}) fusion(bf16[2,8192,1024]{2,1,0:T(8,128)(2,1)} %param.28), kind=kLoop, calls=%fused_computation.9 | loop fusion | bytes 67108864 | tf_op jit(solution)/shard_map/dot_general | solution.py:57
  668.8 21.4 %copy.26 = bf16[1024,8192]{1,0:T(8,128)(2,1)} copy(bf16[1024,8192]{0,1:T(8,128)(2,1)} %get-tuple-element.2) | data formatting | bytes 33554432 | tf_op jit(solution)/shard_map/dot_general | solution.py:57
  690.4 0.3 multiply_cosine_fusion
  690.8 4.9 fusion.19
  695.7 0.9 fusion.91
  696.6 8.2 fusion.21
  705.0 2.9 fusion.131
  707.8 1.9 convolution_convert_fusion.1
  709.7 13.6 %fusion.8 = f32[8192,256]{0,1:T(8,128)} fusion(bf16[256,1024]{0,1:T(8,128)(2,1)S(1)} %bitcast.133, bf16[2,1024,8192]{2,1,0:T(8,128)(2,1)} %param.30), kind=kOutput, calls=%fused_computation.10 | convolution fusion | flops 4294967296 | bytes 25690112 | tf_op jit(solution)/shard_map/dot_general | solution.py:93
  723.4 0.6 dynamic-slice_convert_fusion
  724.0 72.3 %reduce-scatter.6.cloned.1.call-done = f32[2048,256]{0,1:T(8,128)} async-done(((f32[8192,256]{0,1:T(8,128)}), f32[2048,256]{0,1:T(8,128)}) %reduce-scatter.6.cloned.1.call-update) | async-done | bytes 2097168 | tf_op jit(solution)/shard_map/reduce_scatter | solution.py:92
  796.3 2.9 multiply_reduce_fusion
  799.2 6.4 psum.22
  805.6 0.7 add_rsqrt_fusion
  806.3 2.5 multiply_convert_fusion
  808.9 21.5 %copy.30 = bf16[1024,8192]{1,0:T(8,128)(2,1)} copy(bf16[1024,8192]{0,1:T(8,128)(2,1)} %get-tuple-element.3) | data formatting | bytes 33554432 | tf_op jit(solution)/shard_map/dot_general | solution.py:57
  830.4 18.8 %fusion.67 = f32[40,5120]{1,0:T(8,128)} fusion(bf16[5120,1280]{1,0:T(8,128)(2,1)} %all-gather.5.cloned.1.call-done, bf16[1280,8192]{1,0:T(8,128)(2,1)} %all-gather.7.cloned.1.call-done, bf16[40,8192]{1,0:T(8,128)(2,1)} %param.31, pred[40]{0:T(512)(128)(4,1)} %copy-done.30, f32[40,1280]{1,0:T(8,128)S(1)} %convolution_add_fusion), kind=kOutput, calls=%fused_computation.84 | convolution fusion | flops 1367162880 | bytes 35758120 | tf_op jit(solution)/shard_map/dot_general | solution.py:119
  849.2 0.3 reduce-scatter.8.cloned.1.call-start
  849.5 4.9 fusion.14
  854.4 0.3 fusion.95
  854.8 0.4 copy-done.19
  855.1 8.3 fusion.16
  863.5 1.0 subtract_convert_fusion
  864.5 3.1 fusion.134
  867.6 2.0 convolution_convert_fusion
  869.6 13.8 %fusion.11 = f32[8192,256]{0,1:T(8,128)} fusion(bf16[256,1024]{0,1:T(8,128)(2,1)S(1)} %bitcast.134, bf16[2,1024,8192]{2,1,0:T(8,128)(2,1)} %param.30), kind=kOutput, calls=%fused_computation.11 | convolution fusion | flops 4294967296 | bytes 25690112 | tf_op jit(solution)/shard_map/dot_general | solution.py:93
  883.4 0.7 copy-done.24
  884.0 1.3 all-reduce.2.cloned.1.call-done
  885.3 2.4 reshape.226
  887.8 1.7 multiply_reduce_fusion.1
  889.5 1.7 fusion.39
  892.0 1.2 fusion.38
  893.1 66.7 %reduce-scatter.8.cloned.1.call-done = f32[2048,256]{0,1:T(8,128)} async-done(((f32[8192,256]{0,1:T(8,128)}), f32[2048,256]{0,1:T(8,128)}) %reduce-scatter.8.cloned.1.call-update) | async-done | bytes 2097168 | tf_op jit(solution)/shard_map/reduce_scatter | solution.py:92
  959.8 3.6 bitcast_add_fusion
  (109 shorter events, 2.5 us)
Async XLA Ops:
  7.2 1.6 copy-start.27
  7.2 1.6 copy-start.29
  7.2 1.6 copy-start.23
  7.2 1.6 copy-start.6
  7.2 188.6 %all-gather.5.cloned.1.call-start = ((), (), s32[]{:S(2)}) async-start(), calls=%async_computation.3 | async-start | bytes 14745600 | tf_op jit(solution)/shard_map/all_gather | solution.py:148
  7.9 589.4 %all-gather.7.cloned.1.call-start = ((), (), s32[]{:S(2)}) async-start(), calls=%async_computation.4 | async-start | bytes 23592960 | tf_op jit(solution)/shard_map/all_gather | solution.py:149
  8.7 627.5 %reduce-scatter.4.cloned.1.call-start = ((), (), s32[]{:S(2)}) async-start(), calls=%async_computation.5 | async-start | bytes 1638400 | tf_op jit(solution)/shard_map/reduce_scatter | solution.py:110
  8.9 194.0 %copy-start.12 = (f32[5120]{0:T(1024)}, f32[5120]{0:T(1024)S(1)}, u32[]{:S(2)}) copy-start(f32[5120]{0:T(1024)S(1)} %mul.308) | copy-start | bytes 61444
  9.8 186.0 %copy-start.16 = (f32[40,4]{1,0:T(8,128)}, f32[40,4]{1,0:T(8,128)S(1)}, u32[]{:S(2)}) copy-start(f32[40,4]{1,0:T(8,128)S(1)} %multiply_reduce_fusion.2) | copy-start | bytes 1924
  9.8 186.0 %copy-start.14 = (f32[40,4]{1,0:T(8,128)}, f32[40,4]{1,0:T(8,128)S(1)}, u32[]{:S(2)}) copy-start(f32[40,4]{1,0:T(8,128)S(1)} %fusion.111) | copy-start | bytes 1924
  10.2 192.7 %copy-start.2 = (f32[5,8,4,1280]{3,1,2,0:T(8,128)}, f32[5,8,4,1280]{3,1,2,0:T(8,128)S(1)}, u32[]{:S(2)}) copy-start(f32[5,8,4,1280]{3,1,2,0:T(8,128)S(1)} %copy.43) | copy-start | bytes 2457604
  10.5 192.4 %copy-start.4 = (f32[5,8,4,1280]{3,1,2,0:T(8,128)}, f32[5,8,4,1280]{3,1,2,0:T(8,128)S(1)}, u32[]{:S(2)}) copy-start(f32[5,8,4,1280]{3,1,2,0:T(8,128)S(1)} %copy.42) | copy-start | bytes 2457604
  202.9 407.3 %copy-start.28 = (bf16[2048]{0:T(1024)(128)(2,1)S(1)}, bf16[2048]{0:T(1024)(128)(2,1)}, u32[]{:S(2)}) copy-start(bf16[2048]{0:T(1024)(128)(2,1)} %param.22) | copy-start | bytes 12292
  202.9 407.3 %copy-start.33 = (s32[40]{0:T(128)S(1)}, s32[40]{0:T(128)}, u32[]{:S(2)}) copy-start(s32[40]{0:T(128)} %param.23) | copy-start | bytes 484
  202.9 407.4 %copy-start.18 = (bf16[2,8192]{1,0:T(2,128)(2,1)S(1)}, bf16[2,8192]{1,0:T(2,128)(2,1)}, u32[]{:S(2)}) copy-start(bf16[2,8192]{1,0:T(2,128)(2,1)} %param.27) | copy-start | bytes 98308
  609.5 81.3 %all-gather.9.cloned.1.call-start = ((), (), s32[]{:S(2)}) async-start(), calls=%async_computation.6 | async-start | bytes 5242880 | tf_op jit(solution)/shard_map/all_gather | solution.py:79
  610.2 58.5 %copy-start.30 = (pred[40]{0:T(512)(128)(4,1)}, pred[40]{0:T(512)(128)(4,1)S(1)}, u32[]{:S(2)}) copy-start(pred[40]{0:T(512)(128)(4,1)S(1)} %iota_compare_fusion.2) | copy-start | bytes 124
  638.2 30.6 %copy-start.1 = (bf16[256,2048]{1,0:T(8,128)(2,1)}, bf16[256,2048]{1,0:T(8,128)(2,1)S(1)}, u32[]{:S(2)}) copy-start(bf16[256,2048]{1,0:T(8,128)(2,1)S(1)} %get-tuple-element.17) | copy-start | bytes 3145732
  645.3 151.0 %reduce-scatter.6.cloned.1.call-start = ((), (), s32[]{:S(2)}) async-start(), calls=%async_computation.7 | async-start | bytes 10485760 | tf_op jit(solution)/shard_map/reduce_scatter | solution.py:92
  668.8 21.4 %copy-start.22 = (s32[1,256]{1,0:T(1,128)S(1)}, s32[1,256]{1,0:T(1,128)}, u32[]{:S(2)}) copy-start(s32[1,256]{1,0:T(1,128)} %param.26) | copy-start | bytes 3076
  690.2 5.5 copy-start.25
  690.4 14.6 %copy-start.20 = (pred[256,256]{0,1:T(8,128)(4,1)}, pred[256,256]{0,1:T(8,128)(4,1)S(1)}, u32[]{:S(2)}) copy-start(pred[256,256]{0,1:T(8,128)(4,1)S(1)} %fusion.54) | copy-start | bytes 196612
  690.7 14.1 %copy-start.8 = (f32[256,64]{0,1:T(8,128)}, f32[256,64]{0,1:T(8,128)S(1)}, u32[]{:S(2)}) copy-start(f32[256,64]{0,1:T(8,128)S(1)} %get-tuple-element.14) | copy-start | bytes 196612
  690.7 14.1 %copy-start.10 = (f32[256,64]{0,1:T(8,128)}, f32[256,64]{0,1:T(8,128)S(1)}, u32[]{:S(2)}) copy-start(f32[256,64]{0,1:T(8,128)S(1)} %get-tuple-element.15) | copy-start | bytes 196612
  690.8 5.8 copy-start.32
  723.3 126.2 %all-gather.11.cloned.1.call-start = ((), (), s32[]{:S(2)}) async-start(), calls=%async_computation.8 | async-start | bytes 5242880 | tf_op jit(solution)/shard_map/all_gather | solution.py:79
  796.3 10.0 %copy-start = (f32[2048,256]{0,1:T(8,128)S(1)}, f32[2048,256]{0,1:T(8,128)}, u32[]{:S(2)}) copy-start(f32[2048,256]{0,1:T(8,128)} %reduce-scatter.6.cloned.1.call-done) | copy-start | bytes 6291460
  808.9 76.5 %all-reduce.2.cloned.1.call-start = ((), (), s32[]{:S(2)}) async-start(), calls=%async_computation.10 | async-start | bytes 1638400 | tf_op jit(solution)/shard_map/psum | solution.py:122
  849.2 5.2 copy-start.26
  849.2 110.6 %reduce-scatter.8.cloned.1.call-start = ((), (), s32[]{:S(2)}) async-start(), calls=%async_computation.9 | async-start | bytes 10485760 | tf_op jit(solution)/shard_map/reduce_scatter | solution.py:92
  849.5 5.6 copy-start.31
  854.4 0.7 copy-start.19
  855.1 8.4 copy-start.9
  855.1 8.4 copy-start.11
  855.1 9.3 copy-start.21
  883.3 0.7 copy-start.24
  883.4 6.1 copy-start.17
  883.4 6.2 copy-start.15
  887.8 4.1 copy-start.3
  887.8 4.2 copy-start.5
  887.8 4.2 copy-start.7
  887.8 4.2 copy-start.13
Sparse Core Ops, SparseCore 0:
  10.2 185.5 all-gather.4
  197.3 399.9 all-gather.6
  609.6 26.5 reduce-scatter.3
  645.4 35.5 all-gather.8
  723.5 72.7 reduce-scatter.5
  809.0 35.5 all-gather.10
  849.3 35.9 all-reduce.1
  887.9 71.8 reduce-scatter.7
where the time goes:
time: 972 us; the launch traced here: 970 us
  waiting for transfers between devices  747 us (77%)
  matrix products  103 us (11%)
  local copies, waits for them, and re-layouts  71.5 us (7%)
  other arithmetic  19.9 us (2%)
  between operations  15.4 us (2%)
  blocking collectives  12.2 us (1%)
    all_gather x1, waiting for transfers between devices, local(): lax.all_gather(w_out, 'dp', axis=1, tiled=True)  394 us
    all_gather x1, waiting for transfers between devices, local(): lax.all_gather(w_in, 'dp', axis=0, tiled=True)  185 us
    reduce_scatter x2, waiting for transfers between devices, section_features(): lax.psum_scatter(lax.dot_general(o_local, attended, (((0,), (1,)), ((), (...  139 us
    dot_general x3, local copies, waits for them, and re-layouts, attend(): jnp.dot(normed, q_local, preferred_element_type=jnp.float32)  66.1 us
    dot_general x2, matrix products, section_features(): lax.dot_general(o_local, attended, (((0,), (1,)), ((), ())), preferred_el...  27.3 us
    reduce_scatter x1, waiting for transfers between devices, merger_front(): lax.psum_scatter(partial_out, ('sec', 'mp'), scatter_dimension=1, tiled=T...  25.7 us
  transfers between devices with their start and end apart: 8, of which 6 were waited for; matrix products, arithmetic and copies ran while one was open for 14% of the time, Pallas kernels for 0%

commit v1 on v0

--- a/solution.py
+++ b/solution.py
@@ -100,30 +100,116 @@
     return rows_local + summed.T
 
 
-def merger_front(patch_rows, ln_gain, ln_shift, w_in_full, b_in, w_out_full, b_out):
-    normed = group_norm(patch_rows, ln_gain, ln_shift).astype(jnp.bfloat16)
-    pre_act = jnp.dot(normed, w_in_full, preferred_element_type=jnp.float32) + b_in.astype(
-        jnp.float32
-    )
-    hidden_units = gelu_exact(pre_act).astype(jnp.bfloat16)
-    partial_out = jnp.dot(hidden_units, w_out_full, preferred_element_type=jnp.float32)
-    merged = lax.psum_scatter(
-        partial_out, ("sec", "mp"), scatter_dimension=1, tiled=True
-    ) + b_out.astype(jnp.float32)
-    return (merged.astype(jnp.bfloat16), pre_act)
-
-
-def merger_back(patch_rows, pre_act, hidden_grads, ln_gain, ln_shift, w_in_full):
-    _, pull_gelu = jax.vjp(gelu_exact, pre_act)
-    pre_grads = pull_gelu(hidden_grads)[0].astype(jnp.bfloat16)
-    normed_grads = lax.dot_general(
-        pre_grads, w_in_full, (((1,), (1,)), ((), ())), preferred_element_type=jnp.float32
-    )
-    normed_grads = lax.psum(normed_grads, ("sec", "mp"))
+def swap(values, axis, mask):
+    size = lax.axis_size(axis)
+    return lax.ppermute(values, axis, [(i, i ^ mask) for i in range(size)])
+
+
+def spread_rows(values, parts):
+    return lax.all_to_all(values, "dp", split_axis=0, concat_axis=0, tiled=True).reshape(
+        (parts, -1) + values.shape[1:]
+    )
+
+
+def merger(patches, ln_gain, ln_shift, w_in, b_in, w_out, live_slot, count, grad_rows, packed_rows):
+    owners = lax.axis_size("dp")
+    group = lax.axis_size(("sec", "mp"))
+    slots = patches.shape[0]
+    in_share, hidden_share = w_in.shape
+    out_share = w_out.shape[1]
+    share = in_share + out_share
+
+    normed = group_norm(patches, ln_gain, ln_shift).astype(jnp.bfloat16)
+    slot_grads = jnp.where(live_slot[:, None], grad_rows, jnp.zeros_like(grad_rows))
+    rows = jnp.concatenate(
+        [normed.reshape(slots, owners, in_share), slot_grads.reshape(slots, owners, out_share)],
+        axis=2,
+    ).transpose(1, 0, 2)
+    count_rows = jnp.broadcast_to(count.astype(jnp.bfloat16), (owners, 8, share))
+    received = lax.all_to_all(
+        jnp.concatenate([rows, count_rows], axis=1), "dp", split_axis=0, concat_axis=0, tiled=True
+    )
+    counts = received[:, slots, 0].astype(jnp.int32)
+    owner_index = jnp.arange(owners, dtype=jnp.int32)
+    offsets = jnp.sum(jnp.where(owner_index[None, :] < owner_index[:, None], counts[None, :], 0), axis=1)
+    slot_index = jnp.arange(slots, dtype=jnp.int32)
+    target = jnp.where(
+        slot_index[None, :] < counts[:, None], offsets[:, None] + slot_index[None, :], -1
+    ).reshape(-1)
+    pack = (jnp.arange(packed_rows, dtype=jnp.int32)[:, None] == target[None, :]).astype(jnp.bfloat16)
+    packed = jnp.dot(
+        pack, received[:, :slots].reshape(owners * slots, share), preferred_element_type=jnp.float32
+    ).astype(jnp.bfloat16)
+
+    pre_part = jnp.dot(packed[:, :in_share], w_in, preferred_element_type=jnp.float32)
+    grad_part = lax.dot_general(
+        packed[:, in_share:], w_out, (((1,), (1,)), ((), ())), preferred_element_type=jnp.float32
+    )
+    parts = jnp.concatenate([pre_part, grad_part], axis=1).astype(jnp.bfloat16)
+    chunk = packed_rows // owners
+    parts = lax.all_to_all(
+        parts.reshape(owners, chunk, 2 * hidden_share), "dp", split_axis=0, concat_axis=0, tiled=True
+    )
+    sums = jnp.sum(parts.astype(jnp.float32), axis=0)
+    pre_act = sums[:, :hidden_share] + b_in.astype(jnp.float32)
+    hidden_units, pull_gelu = jax.vjp(gelu_exact, pre_act)
+    pre_grads = pull_gelu(sums[:, hidden_share:])[0]
+    both = jnp.concatenate([hidden_units, pre_grads], axis=1).astype(jnp.bfloat16)
+    both = lax.all_to_all(
+        jnp.broadcast_to(both[None], (owners, chunk, 2 * hidden_share)),
+        "dp",
+        split_axis=0,
+        concat_axis=0,
+        tiled=True,
+    ).reshape(packed_rows, 2 * hidden_share)
+    merged_part = jnp.dot(both[:, :hidden_share], w_out, preferred_element_type=jnp.float32)
+    back_part = lax.dot_general(
+        both[:, hidden_share:], w_in, (((1,), (1,)), ((), ())), preferred_element_type=jnp.float32
+    )
+    tail = jnp.concatenate(
+        [
+            merged_part.astype(jnp.bfloat16).reshape(packed_rows, group, out_share // group),
+            back_part.astype(jnp.bfloat16).reshape(packed_rows, group, in_share // group),
+        ],
+        axis=2,
+    ).reshape(packed_rows, group * (share // group))
+    tail = lax.dot_general(
+        pack, tail, (((0,), (0,)), ((), ())), preferred_element_type=jnp.float32
+    ).astype(jnp.bfloat16)
+    tail = tail.reshape(owners * slots, group, share // group).transpose(1, 0, 2)
+    me = lax.axis_index(("sec", "mp"))
+    parts_now = tail.astype(jnp.float32)
+    index = jnp.arange(group, dtype=jnp.int32) ^ me
+    parts_now = jnp.take(parts_now, index, axis=0)
+    mask = 1
+    while mask < group:
+        pairs = parts_now.reshape(-1, 2, owners * slots, share // group)
+        received = swap(pairs[:, 1].astype(jnp.bfloat16), ("sec", "mp"), mask)
+        parts_now = pairs[:, 0] + received.astype(jnp.float32)
+        mask *= 2
+    mine = parts_now.reshape(owners, slots, share // group).astype(jnp.bfloat16)
+    mine = lax.all_to_all(mine, "dp", split_axis=0, concat_axis=0, tiled=True)
+    gathered = mine[None]
+    mask = group // 2
+    while mask >= 1:
+        gathered = jnp.concatenate([gathered, swap(gathered, ("sec", "mp"), mask)], axis=0)
+        mask //= 2
+    order = [0]
+    mask = group // 2
+    while mask >= 1:
+        order = order + [i ^ mask for i in order]
+        mask //= 2
+    place_of = [0] * group
+    for where_now, relative in enumerate(order):
+        place_of[relative] = where_now
+    gathered = jnp.take(gathered, jnp.asarray(place_of, jnp.int32)[index], axis=0)
+    gathered = gathered.transpose(2, 1, 0, 3)
+    merged = gathered[..., : out_share // group].reshape(slots, owners * out_share)
+    normed_grads = gathered[..., out_share // group :].reshape(slots, owners * in_share)
     _, pull_norm = jax.vjp(
-        lambda values: group_norm(values, ln_gain, ln_shift), patch_rows.astype(jnp.float32)
-    )
-    return pull_norm(normed_grads)[0]
+        lambda values: group_norm(values, ln_gain, ln_shift), patches.astype(jnp.float32)
+    )
+    return merged, pull_norm(normed_grads.astype(jnp.float32))[0]
 
 
 def local(
@@ -144,22 +230,26 @@
     o_weight,
     grad_rows,
 ):
-    w_in_full, w_out_full = (
-        lax.all_gather(w_in, "dp", axis=0, tiled=True),
-        lax.all_gather(w_out, "dp", axis=1, tiled=True),
-    )
     slot_count = patches.shape[0]
-    tokens = text_rows.shape[0]
+    tokens, share = text_rows.shape
     slot_index = jnp.arange(slot_count, dtype=jnp.int32)
     live_slot = slot_index < image_counts[0]
-    slot_grads = jnp.where(live_slot[:, None], grad_rows, jnp.zeros_like(grad_rows))
-    hidden_grads = lax.dot_general(
-        slot_grads, w_out_full, (((1,), (1,)), ((), ())), preferred_element_type=jnp.float32
-    )
-    merged_local, pre_act = merger_front(
-        patches, ln_gain, ln_shift, w_in_full, b_in, w_out_full, b_out
-    )
-    patch_grads = merger_back(patches, pre_act, hidden_grads, ln_gain, ln_shift, w_in_full)
+    merged, patch_grads = merger(
+        patches,
+        ln_gain,
+        ln_shift,
+        w_in,
+        b_in,
+        w_out,
+        live_slot,
+        image_counts[0],
+        grad_rows,
+        lax.axis_size("dp") * (tokens // 16),
+    )
+    merged_local = lax.dynamic_slice_in_dim(
+        merged, lax.axis_index(("sec", "mp")) * share, share, 1
+    ).astype(jnp.float32)
+    merged_local = (merged_local + b_out.astype(jnp.float32)).astype(jnp.bfloat16)
     token_index = jnp.arange(tokens, dtype=jnp.int32)
     select = (place[:, None] == token_index[None, :]) & live_slot[:, None]
     is_image = jnp.any(select, axis=0)

time: 972 us -> 494 us (0.51)
  waiting for transfers between devices: 747 us -> 201 us
  blocking collectives: 12.2 us -> 50.4 us
  local copies, waits for them, and re-layouts: 71.5 us -> 99.7 us
  matrix products: 103 us -> 82.7 us
  starting transfers between devices: 0.72 us -> 15.7 us
    all_gather x2 -> x0, waiting for transfers between devices: 580 us -> none  [the longest x1 394 us: local(): lax.all_gather(w_out, 'dp', axis=1, tiled=True)]
    all_to_all x0 -> x3, waiting for transfers between devices: none -> 42.8 us  [the longest x1 16.6 us: merger(): lax.all_to_all(jnp.broadcast_to(both[None], (owners, chunk, 2 * hidden_sh...]
    all_to_all x0 -> x1, blocking collectives: none -> 37.7 us  [merger(): lax.all_to_all(jnp.concatenate([rows, count_rows], axis=1), 'dp', split_a...]
    dot_general x3 -> x6, matrix products: 38 us -> 7.29 us  [the longest x1 2.83 us: merger(): lax.dot_general(both[:, hidden_share:], w_in, (((1,), (1,)), ((), ())), p...]
    reduce_scatter x1 -> x0, waiting for transfers between devices: 25.7 us -> none  [merger_front(): lax.psum_scatter(partial_out, ('sec', 'mp'), scatter_dimension=1, tiled=T...]
    ppermute x0 -> x4, waiting for transfers between devices: none -> 15.9 us  [swap(): return lax.ppermute(values, axis, [(i, i ^ mask) for i in range(size)])]
    all_gather x2, waiting for transfers between devices: 0.04 us -> 14.1 us  [gather_features(): return lax.all_gather(rows_local, ('sec', 'mp'), axis=1, tiled=True)]
    dot_general x2, matrix products: 16.5 us -> 29.9 us  [attend(): jnp.dot(normed, q_local, preferred_element_type=jnp.float32)]
  transfers between devices with their start and end apart: 8 -> 11, of which waited for: 6 -> 10; matrix products, arithmetic and copies ran while one was open for 14% -> 17% of each run, Pallas kernels for 0% -> 0%
where the time goes in v1:
time: 494 us; the launch traced here: 489 us
  waiting for transfers between devices  201 us (41%)
  local copies, waits for them, and re-layouts  99.7 us (20%)
  matrix products  82.7 us (17%)
  blocking collectives  50.4 us (10%)
  other arithmetic  23.8 us (5%)
  starting transfers between devices  15.7 us (3%)
  between operations  15.5 us (3%)
    reduce_scatter x2, waiting for transfers between devices, section_features(): lax.psum_scatter(lax.dot_general(o_local, attended, (((0,), (1,)), ((), (...  128 us
    dot_general x3, local copies, waits for them, and re-layouts, attend(): jnp.dot(normed, q_local, preferred_element_type=jnp.float32)  66.1 us
    all_to_all x1, blocking collectives, merger(): lax.all_to_all(jnp.concatenate([rows, count_rows], axis=1), 'dp', split_a...  37.7 us
    dot_general x2, matrix products, attend(): jnp.dot(normed, q_local, preferred_element_type=jnp.float32)  29.9 us
    dot_general x2, matrix products, section_features(): lax.dot_general(o_local, attended, (((0,), (1,)), ((), ())), preferred_el...  27.2 us
    all_to_all x1, waiting for transfers between devices, merger(): lax.all_to_all(jnp.broadcast_to(both[None], (owners, chunk, 2 * hidden_sh...  16.6 us
    all_to_all x1, waiting for transfers between devices, merger(): lax.all_to_all(parts.reshape(owners, chunk, 2 * hidden_share), 'dp', spli...  16.5 us
    ppermute x4, waiting for transfers between devices, swap(): return lax.ppermute(values, axis, [(i, i ^ mask) for i in range(size)])  15.9 us
  transfers between devices with their start and end apart: 11, of which 10 were waited for; matrix products, arithmetic and copies ran while one was open for 17% of the time, Pallas kernels for 0%

profile of v1, /device:TPU:0, one launch (start us, length us, event | category | flops | bytes accessed | tf_op | source)
XLA Modules:
  0.0 488.8 jit_solution(13263538039777772244)
XLA Ops:
  8.0 1.2 broadcast_select_fusion.1
  10.4 1.4 reshape.391
  17.0 1.3 concatenate.50.clone
  18.3 37.7 %all_to_all.20 = bf16[8,48,1664]{2,1,0:T(8,128)(2,1)S(1)} all-to-all(bf16[8,48,1664]{2,1,0:T(8,128)(2,1)S(1)} %concatenate.50.clone), channel_id=1, replica_groups=mesh['sec'=4,'dp'=8,'mp'=1] {'dp'}, dimensions={0} | all-to-all | bytes 2555904 | tf_op jit(solution)/shard_map/all_to_all | solution.py:129
  57.6 1.2 slice-done
  61.6 4.2 all-to-all-start.1
  65.8 16.5 %all-to-all-done.1 = bf16[8,16,2560]{2,1,0:T(8,128)(2,1)} async-done(((bf16[8,16,2560]{2,1,0:T(8,128)(2,1)}), bf16[8,16,2560]{2,1,0:T(8,128)(2,1)}, u32[]{:S(2)}, u32[]{:S(2)}) %all-to-all-start.1) | async-done | bytes 655392 | tf_op jit(solution)/shard_map/all_to_all | solution.py:150
  84.7 4.2 all-to-all-start.2
  88.9 16.6 %all-to-all-done.2 = bf16[8,16,2560]{2,1,0:T(8,128)(2,1)} async-done(((bf16[8,16,2560]{2,1,0:T(8,128)(2,1)}), bf16[8,16,2560]{2,1,0:T(8,128)(2,1)}, u32[]{:S(2)}, u32[]{:S(2)}) %all-to-all-start.2) | async-done | bytes 655392 | tf_op jit(solution)/shard_map/all_to_all | solution.py:158
  105.6 2.8 convolution_convert_fusion.7
  108.4 2.2 convolution_convert_fusion.6
  113.3 2.1 copy.166
  115.4 2.4 gather_fusion.1
  118.3 2.1 collective-permute-done
  120.6 1.6 collective-permute-start.1
  122.2 8.1 %collective-permute-done.1 = bf16[1,320,416]{1,2,0:T(8,128)(2,1)S(1)} collective-permute-done((bf16[1,320,416]{1,2,0:T(8,128)(2,1)S(1)}, bf16[1,320,416]{1,2,0:T(8,128)(2,1)S(1)}, u32[]{:S(2)}, u32[]{:S(2)}) %collective-permute-start.1) | collective-permute-done | bytes 266272 | tf_op jit(solution)/shard_map/ppermute | solution.py:105
  131.2 3.6 all-to-all-start.3
  135.0 9.6 %all-to-all-done.3 = bf16[8,40,416]{2,1,0:T(8,128)(2,1)S(1)} async-done(((bf16[8,40,416]{2,1,0:T(8,128)(2,1)}), bf16[8,40,416]{2,1,0:T(8,128)(2,1)S(1)}, u32[]{:S(2)}, u32[]{:S(2)}) %all-to-all-start.3) | async-done | bytes 266272 | tf_op jit(solution)/shard_map/all_to_all | solution.py:191
  144.6 1.5 collective-permute-start.2
  147.5 4.2 collective-permute-done.2
  152.4 1.5 collective-permute-done.3
  157.1 1.9 fusion.28
  159.1 6.9 %psum.14 = f32[256]{0:T(256)S(1)} all-reduce(f32[256]{0:T(256)S(1)} %get-tuple-element.18), channel_id=1, replica_groups=mesh['sec'=4,'dp'=8,'mp'=1] {'sec','mp'}, use_global_device_ids=true, to_apply=%region_6.7 | all-reduce | flops 256 | bytes 2048 | tf_op jit(solution)/shard_map/psum | solution.py:84
  166.0 1.3 fusion.30
  167.6 23.3 %slice_bitcast_fusion.1 = (bf16[1024,8192]{0,1:T(8,128)(2,1)}, bf16[1024,8192]{0,1:T(8,128)(2,1)}) fusion(bf16[2,8192,1024]{2,1,0:T(8,128)(2,1)} %param.29), kind=kLoop, calls=%fused_computation.12 | loop fusion | bytes 67108864 | tf_op jit(solution)/shard_map/dot_general | solution.py:57
  190.9 21.3 %copy.144 = bf16[1024,8192]{1,0:T(8,128)(2,1)} copy(bf16[1024,8192]{0,1:T(8,128)(2,1)} %get-tuple-element.4) | data formatting | bytes 33554432 | tf_op jit(solution)/shard_map/dot_general | solution.py:57
  212.9 4.9 fusion.19
  218.1 8.2 %fusion.21 = f32[256,8,128]{0,2,1:T(8,128)S(1)} fusion(bf16[8,128,8192]{2,1,0:T(8,128)(2,1)} %bitcast.175, bf16[256,8192]{1,0:T(8,128)(2,1)S(1)} %copy-done.25), kind=kOutput, calls=%fused_computation.22 | convolution fusion | flops 4294967296 | bytes 22020096 | tf_op jit(solution)/shard_map/dot_general | solution.py:57
  226.4 2.1 fusion.127
  228.5 1.9 convolution_convert_fusion.5
  230.4 13.6 %fusion.8 = f32[8192,256]{0,1:T(8,128)} fusion(bf16[256,1024]{0,1:T(8,128)(2,1)S(1)} %bitcast.201, bf16[2,1024,8192]{2,1,0:T(8,128)(2,1)} %param.31), kind=kOutput, calls=%fused_computation.13 | convolution fusion | flops 4294967296 | bytes 25690112 | tf_op jit(solution)/shard_map/dot_general | solution.py:93
  244.1 71.9 %reduce-scatter.3.cloned.1.call-done = f32[2048,256]{0,1:T(8,128)} async-done(((f32[8192,256]{0,1:T(8,128)}), f32[2048,256]{0,1:T(8,128)}) %reduce-scatter.3.cloned.1.call-update) | async-done | bytes 2097168 | tf_op jit(solution)/shard_map/reduce_scatter | solution.py:92
  316.0 2.4 multiply_reduce_fusion
  318.3 5.8 %psum.15 = f32[256]{0:T(256)S(1)} all-reduce(f32[256]{0:T(256)S(1)} %multiply_reduce_fusion), channel_id=1, replica_groups=mesh['sec'=4,'dp'=8,'mp'=1] {'sec','mp'}, use_global_device_ids=true, to_apply=%region_12.13 | all-reduce | flops 256 | bytes 2048 | tf_op jit(solution)/shard_map/psum | solution.py:84
  324.1 2.5 multiply_convert_fusion
  326.7 21.5 %copy.148 = bf16[1024,8192]{1,0:T(8,128)(2,1)} copy(bf16[1024,8192]{0,1:T(8,128)(2,1)} %get-tuple-element.5) | data formatting | bytes 33554432 | tf_op jit(solution)/shard_map/dot_general | solution.py:57
  348.2 14.1 %all-gather.5.cloned.1.call-done = bf16[256,8192]{1,0:T(8,128)(2,1)} async-done(((bf16[256,2048]{1,0:T(8,128)(2,1)}), bf16[256,8192]{1,0:T(8,128)(2,1)}) %all-gather.5.cloned.1.call-update) | async-done | bytes 4194320 | tf_op jit(solution)/shard_map/all_gather | solution.py:79
  362.4 21.8 %fusion.16 = f32[256,8,128]{0,2,1:T(8,128)S(1)} fusion(bf16[8,128,8192]{2,1,0:T(8,128)(2,1)} %bitcast.176, bf16[256,8192]{1,0:T(8,128)(2,1)} %all-gather.5.cloned.1.call-done), kind=kOutput, calls=%fused_computation.17 | convolution fusion | flops 4294967296 | bytes 22020096 | tf_op jit(solution)/shard_map/dot_general | solution.py:57
  384.3 3.5 fusion.14
  388.1 2.1 fusion.130
  390.2 1.9 convolution_convert_fusion.4
  392.1 13.6 %fusion.11 = f32[8192,256]{0,1:T(8,128)} fusion(bf16[256,1024]{0,1:T(8,128)(2,1)S(1)} %bitcast.202, bf16[2,1024,8192]{2,1,0:T(8,128)(2,1)} %param.31), kind=kOutput, calls=%fused_computation.14 | convolution fusion | flops 4294967296 | bytes 25690112 | tf_op jit(solution)/shard_map/dot_general | solution.py:93
  406.7 2.3 reshape.403
  410.1 2.1 reshape.408
  412.2 2.2 reshape.407
  414.4 1.9 multiply_reduce_fusion.1
  421.4 56.2 %reduce-scatter.5.cloned.1.call-done = f32[2048,256]{0,1:T(8,128)} async-done(((f32[8192,256]{0,1:T(8,128)}), f32[2048,256]{0,1:T(8,128)}) %reduce-scatter.5.cloned.1.call-update) | async-done | bytes 2097168 | tf_op jit(solution)/shard_map/reduce_scatter | solution.py:92
  477.6 4.4 bitcast_add_fusion
  (166 shorter events, 31.6 us)
Async XLA Ops:
  7.2 52.1 %copy-start = (bf16[1280,1024]{1,0:T(8,128)(2,1)S(1)}, bf16[1280,1024]{1,0:T(8,128)(2,1)}, u32[]{:S(2)}) copy-start(bf16[1280,1024]{1,0:T(8,128)(2,1)} %param.22) | copy-start | bytes 7864324
  11.8 2.2 copy-start.24
  11.8 2.2 copy-start.20
  14.0 1.1 copy-start.7
  14.0 1.2 copy-start.11
  14.2 1.6 copy-start.18
  14.4 1.1 copy-start.9
  56.1 1.0 copy-start.16
  57.6 1.2 slice-start
  58.9 1.4 copy-start.14
  60.3 5.5 %copy-start.22 = (bf16[1280]{0:T(1024)(128)(2,1)S(1)}, bf16[1280]{0:T(1024)(128)(2,1)}, u32[]{:S(2)}) copy-start(bf16[1280]{0:T(1024)(128)(2,1)} %param.21) | copy-start | bytes 7684
  61.6 20.7 %all-to-all-start.1 = ((bf16[8,16,2560]{2,1,0:T(8,128)(2,1)}), bf16[8,16,2560]{2,1,0:T(8,128)(2,1)}, u32[]{:S(2)}, u32[]{:S(2)}) async-start(bf16[8,16,2560]{2,1,0:T(8,128)(2,1)} %pad_maximum_fusion.1), calls=%async_computation.1 | async-start | bytes 1310720 | tf_op jit(solution)/shard_map/all_to_all | solution.py:150
  84.7 20.9 %all-to-all-start.2 = ((bf16[8,16,2560]{2,1,0:T(8,128)(2,1)}), bf16[8,16,2560]{2,1,0:T(8,128)(2,1)}, u32[]{:S(2)}, u32[]{:S(2)}) async-start(bf16[8,16,2560]{2,1,0:T(8,128)(2,1)} %broadcast_in_dim.96), calls=%async_computation.2 | async-start | bytes 1310720 | tf_op jit(solution)/shard_map/all_to_all | solution.py:158
  118.2 2.1 collective-permute-start
  120.5 14.4 %copy-start.19 = (bf16[2,8192]{1,0:T(2,128)(2,1)S(1)}, bf16[2,8192]{1,0:T(2,128)(2,1)}, u32[]{:S(2)}) copy-start(bf16[2,8192]{1,0:T(2,128)(2,1)} %param.28) | copy-start | bytes 98308
  120.5 25.6 %copy-start.27 = (s32[40]{0:T(128)S(1)}, s32[40]{0:T(128)}, u32[]{:S(2)}) copy-start(s32[40]{0:T(128)} %param.24) | copy-start | bytes 484
  120.5 26.3 %copy-start.23 = (bf16[2048]{0:T(1024)(128)(2,1)S(1)}, bf16[2048]{0:T(1024)(128)(2,1)}, u32[]{:S(2)}) copy-start(bf16[2048]{0:T(1024)(128)(2,1)} %param.23) | copy-start | bytes 12292
  120.5 26.3 %copy-start.2 = (s32[4]{0:T(128)S(1)}, s32[4]{0:T(128)}, u32[]{:S(2)}) copy-start(s32[4]{0:T(128)} %constant.147.clone) | copy-start | bytes 52
  120.6 9.6 %collective-permute-start.1 = (bf16[1,320,416]{1,2,0:T(8,128)(2,1)S(1)}, bf16[1,320,416]{1,2,0:T(8,128)(2,1)S(1)}, u32[]{:S(2)}, u32[]{:S(2)}) collective-permute-start(bf16[1,320,416]{1,2,0:T(8,128)(2,1)S(1)} %fusion.57), channel_id=1, source_target_pairs={{0,16},{8,24},{16,0},{24,8},{1,17},{9,25},{17,1},{25,9},{2,18},{10... | collective-permute-start | bytes 798728 | tf_op jit(solution)/shard_map/ppermute | solution.py:105
  131.2 13.4 %all-to-all-start.3 = ((bf16[8,40,416]{2,1,0:T(8,128)(2,1)}), bf16[8,40,416]{2,1,0:T(8,128)(2,1)S(1)}, u32[]{:S(2)}, u32[]{:S(2)}) async-start(bf16[8,40,416]{2,1,0:T(8,128)(2,1)} %bitcast.18), calls=%async_computation.3 | async-start | bytes 655360 | tf_op jit(solution)/shard_map/all_to_all | solution.py:191
  134.9 78.0 %all-gather.3.cloned.1.call-start = ((), (), s32[]{:S(2)}) async-start(), calls=%async_computation.6 | async-start | bytes 5242880 | tf_op jit(solution)/shard_map/all_gather | solution.py:79
  144.6 7.1 %collective-permute-start.2 = (bf16[1,8,40,416]{3,2,1,0:T(8,128)(2,1)S(1)}, bf16[1,8,40,416]{3,2,1,0:T(8,128)(2,1)S(1)}, u32[]{:S(2)}, u32[]{:S(2)}) collective-permute-start(bf16[1,8,40,416]{3,2,1,0:T(8,128)(2,1)S(1)} %bitcast.190), channel_id=1, source_target_pairs={{0,16},{8,24},{16,0},{24,8},{1,17},{9,25},{17,1},{25,9},{2,18},{10... | collective-permute-start | bytes 798728 | tf_op jit(solution)/shard_map/ppermute | solution.py:105
  151.8 2.2 collective-permute-start.3
  155.6 1.1 copy-start.5
  159.1 31.8 %copy-start.4 = (bf16[256,2048]{1,0:T(8,128)(2,1)}, bf16[256,2048]{1,0:T(8,128)(2,1)S(1)}, u32[]{:S(2)}) copy-start(bf16[256,2048]{1,0:T(8,128)(2,1)S(1)} %get-tuple-element.19) | copy-start | bytes 3145732
  167.3 148.7 %reduce-scatter.3.cloned.1.call-start = ((), (), s32[]{:S(2)}) async-start(), calls=%async_computation.7 | async-start | bytes 10485760 | tf_op jit(solution)/shard_map/reduce_scatter | solution.py:92
  190.9 21.3 %copy-start.21 = (s32[1,256]{1,0:T(1,128)S(1)}, s32[1,256]{1,0:T(1,128)}, u32[]{:S(2)}) copy-start(s32[1,256]{1,0:T(1,128)} %param.27) | copy-start | bytes 3076
  212.8 5.2 %copy-start.25 = (bf16[256,8192]{1,0:T(8,128)(2,1)S(1)}, bf16[256,8192]{1,0:T(8,128)(2,1)}, u32[]{:S(2)}) copy-start(bf16[256,8192]{1,0:T(8,128)(2,1)} %all-gather.3.cloned.1.call-done) | copy-start | bytes 12582916
  244.0 118.3 %all-gather.5.cloned.1.call-start = ((), (), s32[]{:S(2)}) async-start(), calls=%async_computation.8 | async-start | bytes 5242880 | tf_op jit(solution)/shard_map/all_gather | solution.py:79
  316.0 8.1 %copy-start.3 = (f32[2048,256]{0,1:T(8,128)S(1)}, f32[2048,256]{0,1:T(8,128)}, u32[]{:S(2)}) copy-start(f32[2048,256]{0,1:T(8,128)} %reduce-scatter.3.cloned.1.call-done) | copy-start | bytes 6291460
  326.7 150.9 %reduce-scatter.5.cloned.1.call-start = ((), (), s32[]{:S(2)}) async-start(), calls=%async_computation.9 | async-start | bytes 10485760 | tf_op jit(solution)/shard_map/reduce_scatter | solution.py:92
  362.4 21.9 %copy-start.26 = (bf16[256,8192]{1,0:T(8,128)(2,1)S(1)}, bf16[256,8192]{1,0:T(8,128)(2,1)}, u32[]{:S(2)}) copy-start(bf16[256,8192]{1,0:T(8,128)(2,1)} %all-gather.5.cloned.1.call-done) | copy-start | bytes 12582916
  405.7 1.0 copy-start.12
  406.7 2.5 copy-start.6
  414.4 2.1 copy-start.15
  417.8 1.4 copy-start.8
  417.8 1.8 copy-start.10
  417.8 2.0 copy-start.13
  417.8 2.5 copy-start.17
  420.3 61.7 %copy-start.1 = (bf16[1280,1024]{1,0:T(8,128)(2,1)S(1)}, bf16[1280,1024]{1,0:T(8,128)(2,1)}, u32[]{:S(2)}) copy-start(bf16[1280,1024]{1,0:T(8,128)(2,1)} %param.22) | copy-start | bytes 7864324
Sparse Core Ops, SparseCore 0:
  167.4 34.5 all-gather.2
  244.2 71.7 reduce-scatter.2
  326.8 35.5 all-gather.4
  405.8 71.7 reduce-scatter.4
